TPU v7x, 32 devices: a whole 2x2x4 slice. The times are simulated.
32 devices in a mesh: groups: 2 (over x), isl: 16 (over z, y, core).
Axes of the slice: x: 2, y: 2, z: 4, core: 2. Of those that a mesh axis runs over, the one named last changes fastest.
Arguments:
- particles: bfloat16 [262144, 256], P(('groups', 'isl')), parts along dimension 0, may hold values from -6 to 6
- noise: bfloat16 [3, 262144, 256], P(None, ('groups', 'isl')), parts along dimension 1, may hold values from -3 to 3
- series: float32 [6, 256], P('groups'), parts along dimension 0, may hold values from -6 to 6
- transition: bfloat16 [256, 256], replicated, may hold values from -0.375 to 0.375
- obs_matrix: bfloat16 [256, 256], replicated, may hold values from -0.375 to 0.375
- precision: float32 [256], replicated, may hold values from 1 to 10
- src_island: int32 [3, 2048, 1], P(None, ('groups', 'isl')), parts along dimension 1, may hold values from 0 to 15; in each aligned block of 32 rows (0 to 31, 32 to 63, ..., all dimensions but the last counted through in order) at most 4 rows name the same one
- src_tile: int32 [3, 2048], P(None, ('groups', 'isl')), parts along dimension 1, may hold values from 0 to 63
- swap_bits: int32 [6], P('groups'), parts along dimension 0, may hold values from 0 to 3, as said below
Outputs:
- cloud: bfloat16 [262144, 256], P(('groups', 'isl')), parts along dimension 0
- first_moment: float32 [6, 256], P('groups'), parts along dimension 0
- second_moment: float32 [6, 256, 256], P('groups', 'isl'), parts along dimension 0
There are 2 independent parts, one for each index of `groups`. A program takes and returns all parts, laid end to end along the dimension named above; an argument that names none is the same for every part. Nothing has to cross between parts.
Inputs may be any that keep to these rules, and one draw needn't show every extreme that they name: `src_island`: within each aligned block of 32 slots (half of one island's slots), no island is named more than 4 times; some island is named exactly that often. `swap_bits`: bits lie below log2(16); the top one occurs in every draw.
All inputs are finite; a program needn't handle non-finite values.
Results may differ from a plain program's by a relative error of at most 0.0085.
Values may be sent and summed in bfloat16 or wider, within the bound.
A program may use at most 128 MiB of HBM per device.

v0:
```python
import functools

import jax
import jax.numpy as jnp
from jax import lax
from jax.experimental import pallas as pl
from jax.experimental.pallas import tpu as pltpu
from jax.sharding import PartitionSpec as P

TILE = 128
STEPS = 3
LANES = 128
CHUNK = 8
MESH = pl.DeviceIdType.MESH


def greet_all(total, me, where):
    barrier = pltpu.get_barrier_semaphore()

    def greet(k, carry):
        pl.semaphore_signal(
            barrier, inc=1, device_id=where(lax.rem(me + k, total)), device_id_type=MESH
        )
        return carry

    lax.fori_loop(1, total, greet, 0)
    pl.semaphore_wait(barrier, total - 1)


def share_kernel(total, islands, table_ref, all_ref, send_sems, recv_sems, own_sem):
    me = lax.axis_index("groups") * islands + lax.axis_index("isl")

    def where(peer):
        return (peer // islands, lax.rem(peer, islands))

    greet_all(total, me, where)

    def remote(k):
        return pltpu.make_async_remote_copy(
            src_ref=table_ref,
            dst_ref=all_ref.at[me],
            send_sem=send_sems.at[k],
            recv_sem=recv_sems.at[k],
            device_id=where(lax.rem(me + k, total)),
            device_id_type=MESH,
        )

    def send(k, carry):
        remote(k).start()
        return carry

    def finish(k, carry):
        remote(k).wait()
        return carry

    lax.fori_loop(1, total, send, 0)
    own = pltpu.make_async_copy(table_ref, all_ref.at[me], own_sem)
    own.start()
    lax.fori_loop(1, total, finish, 0)
    own.wait()


def share_tables(table, groups, islands):
    total = groups * islands
    return pl.pallas_call(
        functools.partial(share_kernel, total, islands),
        out_shape=jax.ShapeDtypeStruct((total,) + table.shape, table.dtype),
        in_specs=[pl.BlockSpec(memory_space=pl.ANY)],
        out_specs=pl.BlockSpec(memory_space=pl.ANY),
        scratch_shapes=[
            pltpu.SemaphoreType.DMA((total,)),
            pltpu.SemaphoreType.DMA((total,)),
            pltpu.SemaphoreType.DMA,
        ],
        compiler_params=pltpu.CompilerParams(collective_id=0, has_side_effects=True),
        name="share_tables",
    )(table)


def exchange_kernel(islands, kinds, *refs):
    count = len(kinds)
    sources, targets = refs[:count], refs[count : 2 * count]
    send_sems, recv_sems, own_sems = refs[2 * count :]
    me = lax.axis_index("isl")
    sibling = me + 1 - 2 * lax.rem(me, 2)
    greet_all(islands, me, lambda peer: {"isl": peer})

    def ends(a, k, peer):
        kind = kinds[a]
        if kind == "peer":
            return sources[a].at[peer], targets[a].at[me]
        if kind == "all":
            return sources[a], targets[a].at[me]
        rows = sources[a].shape[1]
        if kind == "half" and k % 2 == 1:
            rows -= TILE
        return sources[a].at[peer, pl.ds(0, rows)], targets[a].at[me, pl.ds(0, rows)]

    def remote(a, k):
        if kinds[a] == "pair":
            peer, source, target = sibling, sources[a], targets[a]
        else:
            peer = lax.rem(me + k, islands)
            source, target = ends(a, k, peer)
        return pltpu.make_async_remote_copy(
            src_ref=source,
            dst_ref=target,
            send_sem=send_sems.at[a, k],
            recv_sem=recv_sems.at[a, k],
            device_id={"isl": peer},
            device_id_type=MESH,
        )

    def own(a):
        source, target = ends(a, 0, me)
        return pltpu.make_async_copy(source, target, own_sems.at[a])

    plans = [
        (a, k)
        for k in range(1, islands)
        for a in range(count)
        if (kinds[a] != "pair" or k == 1)
        and not (kinds[a] == "half" and k % 2 == 1 and sources[a].shape[1] == TILE)
    ]
    for a, k in plans:
        remote(a, k).start()
    kept = [a for a in range(count) if kinds[a] != "pair"]
    for a in kept:
        own(a).start()
    for a, k in plans:
        remote(a, k).wait()
    for a in kept:
        own(a).wait()


def exchange(arrays, kinds, shapes, islands, collective_id, name):
    count = len(arrays)
    return pl.pallas_call(
        functools.partial(exchange_kernel, islands, kinds),
        out_shape=[jax.ShapeDtypeStruct(dims, x.dtype) for x, dims in zip(arrays, shapes)],
        in_specs=[pl.BlockSpec(memory_space=pl.ANY)] * count,
        out_specs=[pl.BlockSpec(memory_space=pl.ANY)] * count,
        scratch_shapes=[
            pltpu.SemaphoreType.DMA((count, islands)),
            pltpu.SemaphoreType.DMA((count, islands)),
            pltpu.SemaphoreType.DMA((count,)),
        ],
        compiler_params=pltpu.CompilerParams(collective_id=collective_id, has_side_effects=True),
        name=name,
    )(*arrays)


def fetch(first_ref, second_ref, index, target, sem):
    split = first_ref.shape[0]

    @pl.when(index < split)
    def _():
        pltpu.make_async_copy(first_ref.at[index], target, sem).start()

    @pl.when(index >= split)
    def _():
        pltpu.make_async_copy(second_ref.at[index - split], target, sem).start()


def filter_kernel(source_ref, send_ref, spare_ref, first_ref, other_ref, *refs):
    noise_ref, series_ref, transition_ref, obs_ref, precision_ref = refs[:5]
    packed_ref, excess_ref, second_ref, stats_ref, fetched, moved, fetch_sems, sem = refs[5:]
    i = pl.program_id(0)

    def prefetch(chunk, slot):
        for t in range(CHUNK):
            index = source_ref[chunk * CHUNK + t]
            fetch(first_ref, other_ref, index, fetched.at[slot, t], fetch_sems.at[slot])

    now = lax.rem(i, 2)

    @pl.when(i == 0)
    def _():
        prefetch(0, 0)

    @pl.when(i + 1 < pl.num_programs(0))
    def _():
        prefetch(i + 1, 1 - now)

    pltpu.make_async_copy(fetched.at[now], fetched.at[now], fetch_sems.at[now]).wait()
    width = transition_ref.shape[0]

    @pl.when(i == 0)
    def _():
        second_ref[...] = jnp.zeros_like(second_ref)
        stats_ref[...] = jnp.zeros_like(stats_ref)

    cloud = fetched[now].reshape(CHUNK * TILE, width)
    propagated = (
        jnp.dot(cloud, transition_ref[...], preferred_element_type=jnp.float32)
        + noise_ref[0].astype(jnp.float32)
    ).astype(jnp.bfloat16)
    moved[pl.ds(i * CHUNK, CHUNK)] = propagated.reshape(CHUNK, TILE, width)
    innovation = series_ref[...] - jnp.dot(
        propagated, obs_ref[...], preferred_element_type=jnp.float32
    )
    misfit = jnp.mean(innovation * innovation * precision_ref[...], axis=1, keepdims=True)
    likelihood = jnp.exp(-0.5 * misfit)
    scaled = propagated.astype(jnp.float32) * likelihood
    sums = jnp.sum(scaled, axis=0, keepdims=True)
    pieces = width // LANES
    for c in range(pieces):
        stats_ref[c : c + 1, :] += sums[:, c * LANES : (c + 1) * LANES]
    stats_ref[pieces : pieces + 1, :] += jnp.broadcast_to(
        jnp.sum(likelihood, axis=0, keepdims=True), (1, LANES)
    )
    second_ref[...] += lax.dot_general(
        scaled.astype(jnp.bfloat16),
        propagated,
        (((0,), (0,)), ((), ())),
        preferred_element_type=jnp.float32,
    )

    @pl.when(i == pl.num_programs(0) - 1)
    def _():
        def pack(k, carry):
            pltpu.make_async_copy(moved.at[send_ref[k]], packed_ref.at[k], sem.at[0]).start()
            return carry

        def pack_excess(k, carry):
            pltpu.make_async_copy(moved.at[spare_ref[k]], excess_ref.at[k], sem.at[1]).start()
            return carry

        lax.fori_loop(0, packed_ref.shape[0], pack, 0, unroll=8)
        lax.fori_loop(0, excess_ref.shape[0], pack_excess, 0, unroll=8)
        pltpu.make_async_copy(packed_ref, packed_ref, sem.at[0]).wait()
        pltpu.make_async_copy(excess_ref, excess_ref, sem.at[1]).wait()


def filter_step(
    step, first, other, source, send, spare, noise, series, transition, obs_matrix, precision
):
    width = transition.shape[0]
    tile_count = source.shape[0]
    rows = CHUNK * TILE
    whole = lambda i, *_: (0, 0)
    matmuls = 3 * 2 * tile_count * TILE * width * width
    return pl.pallas_call(
        filter_kernel,
        grid_spec=pltpu.PrefetchScalarGridSpec(
            num_scalar_prefetch=3,
            grid=(tile_count // CHUNK,),
            in_specs=[
                pl.BlockSpec(memory_space=pl.ANY),
                pl.BlockSpec(memory_space=pl.ANY),
                pl.BlockSpec((1, rows, width), lambda i, *_: (step, i, 0)),
                pl.BlockSpec((1, width), whole),
                pl.BlockSpec((width, width), whole),
                pl.BlockSpec((width, width), whole),
                pl.BlockSpec((1, width), whole),
            ],
            out_specs=[
                pl.BlockSpec(memory_space=pl.ANY),
                pl.BlockSpec(memory_space=pl.ANY),
                pl.BlockSpec((width, width), whole),
                pl.BlockSpec((8, LANES), whole),
            ],
            scratch_shapes=[
                pltpu.VMEM((2, CHUNK, TILE, width), jnp.bfloat16),
                pltpu.VMEM((tile_count, TILE, width), jnp.bfloat16),
                pltpu.SemaphoreType.DMA((2,)),
                pltpu.SemaphoreType.DMA((2,)),
            ],
        ),
        out_shape=[
            jax.ShapeDtypeStruct((send.shape[0], TILE, width), jnp.bfloat16),
            jax.ShapeDtypeStruct((spare.shape[0], TILE, width), jnp.bfloat16),
            jax.ShapeDtypeStruct((width, width), jnp.float32),
            jax.ShapeDtypeStruct((8, LANES), jnp.float32),
        ],
        compiler_params=pltpu.CompilerParams(vmem_limit_bytes=40 * 1024 * 1024),
        cost_estimate=pl.CostEstimate(
            flops=matmuls, bytes_accessed=5 * tile_count * TILE * width * 2, transcendentals=0
        ),
        name="filter_step",
    )(source, send, spare, first, other, noise, series, transition, obs_matrix, precision)


def place_kernel(source_ref, first_ref, other_ref, out_ref, fetched, sems):
    i = pl.program_id(0)

    def prefetch(chunk, slot):
        for t in range(CHUNK):
            index = source_ref[chunk * CHUNK + t]
            fetch(first_ref, other_ref, index, fetched.at[slot, t], sems.at[slot])

    now = lax.rem(i, 2)

    @pl.when(i == 0)
    def _():
        prefetch(0, 0)

    @pl.when(i + 1 < pl.num_programs(0))
    def _():
        prefetch(i + 1, 1 - now)

    pltpu.make_async_copy(fetched.at[now], fetched.at[now], sems.at[now]).wait()
    out_ref[...] = fetched[now]


def place(first, other, source, name):
    tile = first.shape[1:]
    return pl.pallas_call(
        place_kernel,
        grid_spec=pltpu.PrefetchScalarGridSpec(
            num_scalar_prefetch=1,
            grid=(source.shape[0] // CHUNK,),
            in_specs=[pl.BlockSpec(memory_space=pl.ANY)] * 2,
            out_specs=pl.BlockSpec((CHUNK,) + tile, lambda i, *_: (i, 0, 0)),
            scratch_shapes=[
                pltpu.VMEM((2, CHUNK) + tile, first.dtype),
                pltpu.SemaphoreType.DMA((2,)),
            ],
        ),
        out_shape=jax.ShapeDtypeStruct(source.shape + tile, first.dtype),
        compiler_params=pltpu.CompilerParams(vmem_limit_bytes=16 * 1024 * 1024),
        name=name,
    )(source, first, other)


def swap_upper(parents, bits, islands, halfway):
    upper = parents[:, :, halfway:]
    swapped = upper
    for bit in range(max(islands.bit_length() - 1, 1)):
        span = 1 << bit
        flipped = upper.reshape(-1, islands // (2 * span), 2, span, halfway)[:, :, ::-1]
        swapped = jnp.where((bits == bit)[:, None, None], flipped.reshape(upper.shape), swapped)
    return jnp.concatenate([parents[:, :, :halfway], swapped], axis=2)


def plan(tables, bits, group, me, islands, tile_count, direct, capacity):
    groups = bits.shape[0]
    spare = capacity - direct
    wanted = swap_upper(
        tables.reshape(groups * STEPS, islands, tile_count),
        bits.reshape(groups * STEPS),
        islands,
        tile_count // 2,
    )
    island_of = wanted // tile_count
    ids = jnp.arange(islands, dtype=jnp.int32)
    counts = jnp.sum((island_of[:, :, None, :] == ids[:, None]).astype(jnp.int32), axis=3)
    over = jnp.maximum(counts - direct, 0)
    by_chip = jnp.sum(over.reshape(groups, STEPS, islands, islands // 2, 2), axis=4)
    need = jnp.max(by_chip, axis=(0, 2, 3))

    mine = lambda x: lax.dynamic_index_in_dim(
        x.reshape((groups, STEPS) + x.shape[1:]), group, 0, keepdims=False
    )
    island, tile, over = mine(island_of), mine(wanted % tile_count), mine(over)
    before = jnp.arange(tile_count)[:, None] < jnp.arange(tile_count)[None, :]
    matches = island == me
    position = jnp.dot(
        matches.astype(jnp.bfloat16).reshape(STEPS * islands, tile_count),
        before.astype(jnp.bfloat16),
        preferred_element_type=jnp.float32,
    ).reshape(matches.shape)
    ranks = jnp.arange(capacity, dtype=jnp.float32)
    chosen = matches[:, :, None, :] & (position[:, :, None, :] == ranks[None, None, :, None])
    send = jnp.sum(jnp.where(chosen, tile[:, :, None, :], 0), axis=3)

    core = me % 2
    of_even = lax.dynamic_index_in_dim(over, me - core, 2, keepdims=False)[:, :, None]
    order = 2 * jnp.arange(spare, dtype=jnp.int32)[None, :] + ((core + ids) % 2)[:, None]
    from_odd = (order[None] >= of_even).astype(jnp.int32)
    rank = jnp.clip(order[None] - from_odd * of_even, 0, spare - 1)
    carried = (from_odd != core).astype(jnp.int32) * (islands * spare) + ids[:, None] * spare + rank

    own = lax.dynamic_index_in_dim(island, me, 1, keepdims=False)
    same = (own[:, :, None] == own[:, None, :]) & before[None]
    own_rank = jnp.sum(same.astype(jnp.int32), axis=1)
    to_me = lax.dynamic_index_in_dim(over, me, 1, keepdims=False)
    even_over = jnp.pad(to_me[:, :-1], ((0, 0), (1, 0))) * (ids % 2)
    offset = jnp.sum(jnp.where(own[:, :, None] == ids, even_over[:, None, :], 0), axis=2)
    later = own_rank - direct + offset
    carrier = own - own % 2 + (later + me) % 2
    source = jnp.where(
        own_rank < direct,
        own * direct + own_rank,
        islands * direct + carrier * spare + later // 2,
    )
    return (
        need,
        send[:, :, :direct].reshape(STEPS, -1),
        send[:, :, direct:].reshape(STEPS, -1),
        carried,
        source,
    )


def local(
    particles, noise, series, transition, obs_matrix, precision, src_island, src_tile, swap_bits
):
    groups, islands = lax.axis_size("groups"), lax.axis_size("isl")
    group, me = lax.axis_index("groups"), lax.axis_index("isl")
    row_count, width = particles.shape
    tile_count = row_count // TILE
    capacity = 2 * max(2, tile_count // islands)
    direct = capacity // 2
    spare = capacity - direct
    table = src_island[:, :, 0] * tile_count + src_tile
    table = jnp.concatenate([table, swap_bits[:, None]], axis=1)
    table = jnp.pad(table, ((0, 8 - STEPS), (0, LANES - 1 - tile_count)))
    tables = share_tables(table, groups, islands).reshape(groups, islands, 8, LANES)
    bits = tables[:, 0, :STEPS, tile_count]
    parents = jnp.swapaxes(tables[:, :, :STEPS, :tile_count], 1, 2)
    need, send, excess_of, carried, source = plan(
        parents, bits, group, me, islands, tile_count, direct, capacity
    )
    first = other = particles.reshape(tile_count, TILE, width)
    slot = jnp.arange(tile_count, dtype=jnp.int32)
    band = width // islands
    pieces = width // LANES
    moment_type = jnp.bfloat16 if band % 16 == 0 else jnp.float32
    levels = [spare, spare + 1, spare + 2, 2 * spare]
    levels = sorted(set(min(x, 2 * spare) for x in levels))

    def second_exchange(number, excess, of_pair, chosen):
        level = levels[number]
        most = (level + 1) // 2
        packed = place(excess, of_pair, chosen[:, :most].reshape(-1), "pack_spare")
        return exchange(
            [packed.reshape(islands, most * TILE, width)],
            ["half" if level % 2 else "peer_rows"],
            [(islands, spare * TILE, width)],
            islands,
            2 + number,
            "exchange_spare",
        )[0]

    firsts, seconds = [], []
    for step in range(STEPS):
        packed, excess, second, stats = filter_step(
            step,
            first,
            other,
            slot,
            send[step],
            excess_of[step],
            noise,
            series[step : step + 1],
            transition,
            obs_matrix,
            precision[None, :],
        )
        incoming, of_pair, bands, all_stats = exchange(
            [
                packed.reshape(islands, direct * TILE, width),
                excess,
                second.reshape(islands, band, width).astype(moment_type),
                stats,
            ],
            ["peer", "pair", "peer", "all"],
            [
                (islands, direct * TILE, width),
                excess.shape,
                (islands, band, width),
                (islands,) + stats.shape,
            ],
            islands,
            1,
            "exchange_tiles",
        )
        level = sum((need[step] > x).astype(jnp.int32) for x in levels[:-1])
        later = lax.switch(
            level,
            [functools.partial(second_exchange, number) for number in range(len(levels))],
            excess,
            of_pair,
            carried[step],
        )
        first = incoming.reshape(islands * direct, TILE, width)
        other = later.reshape(islands * spare, TILE, width)
        slot = source[step]
        total = jnp.sum(all_stats, axis=0)
        firsts.append(total[:pieces].reshape(width) / total[pieces, 0])
        seconds.append(jnp.sum(bands.astype(jnp.float32), axis=0) / total[pieces, 0])
    cloud = place(first, other, slot, "place_tiles").reshape(row_count, width)
    return (cloud, jnp.stack(firsts), jnp.stack(seconds))


def solution(mesh):
    return jax.shard_map(
        local,
        mesh=mesh,
        in_specs=(
            P(("groups", "isl"), None),
            P(None, ("groups", "isl"), None),
            P("groups", None),
            P(),
            P(),
            P(),
            P(None, ("groups", "isl"), None),
            P(None, ("groups", "isl")),
            P("groups"),
        ),
        out_specs=(P(("groups", "isl"), None), P("groups", None), P("groups", "isl", None)),
        check_vma=False,
    )
```

profile of v0, /device:TPU:13, one launch (start us, length us, event | category | flops | bytes accessed | tf_op | source)
XLA Modules:
  0.0 620.6 jit_solution(7297995737017805715)
XLA Ops:
  3.7 10.3 %share_tables.1 = s32[32,8,128]{2,1,0:T(8,128)} custom-call(s32[8,128]{1,0:T(8,128)} %pad.8.table_ref), custom_call_target="tpu_custom_call" | custom-call | tf_op jit(solution)/shard_map/share_tables/pallas_call | solution.py:65
  14.8 0.9 slice.166
  16.7 1.7 convert_reduce_fusion
  26.1 0.9 select_reduce_fusion
  27.6 2.2 copy-done
  29.8 0.9 copy-done.19
  30.7 0.9 copy-done.21
  32.3 23.8 %filter_step.3 = (bf16[64,128,256]{2,1,0:T(8,128)(2,1)S(1)}, bf16[64,128,256]{2,1,0:T(8,128)(2,1)}, f32[256,256]{1,0:T(8,128)S(1)}, f32[8,128]{1,0:T(8,128)S(1)}) custom-call(s32[64]{0:T(128)S(1)} %iota.50.source_ref, s32[64]{0:T(128)S(1)} %squeeze.100.send_ref, s32[64]{0:T(128)S(1)} %squeeze.101.spare_ref, bf16[64,128,256]{2,1,0:T(8,128)(2,1)S(1)} %bitcast.118, ...), custom_call_target="tpu_custom_call" | custom-call | flops 3221225472 | bytes 20971520 | tf_op jit(solution)/shard_map/filter_step/pallas_call | solution.py:243
  56.1 2.0 copy-done.18
  58.7 100.6 %exchange_tiles.3 = (bf16[16,512,256]{2,1,0:T(8,128)(2,1)}, bf16[64,128,256]{2,1,0:T(8,128)(2,1)}, bf16[16,16,256]{2,1,0:T(8,128)(2,1)}, f32[16,8,128]{2,1,0:T(8,128)}) custom-call(bf16[16,512,256]{2,1,0:T(8,128)(2,1)} %bitcast.137, bf16[64,128,256]{2,1,0:T(8,128)(2,1)} %get-tuple-element.163.refs_1_, bf16[16,16,256]{2,1,0:T(8,128)(2,1)} %bitcast.159, ...), custom_call_target="tpu_custom_call" | custom-call | tf_op jit(solution)/shard_map/exchange_tiles/pallas_call | solution.py:138
  159.4 54.4 %conditional.3 = (bf16[64,128,256]{2,1,0:T(8,128)(2,1)}) conditional(s32[]{:T(128)} %bitcast.62, (s32[1,16,4]{2,1,0:T(8,128)S(1)}, bf16[64,128,256]{2,1,0:T(8,128)(2,1)}, bf16[64,128,256]{2,1,0:T(8,128)(2,1)}) %tuple.56, (s32[1,16,4]{2,1,0:T(8,128)S(1)}, bf16[64,128,256]{2,1,0:T(8,128)(2,1)}, ...), branch_computations={%region_6.7_spmd, %region_7.8_spmd, %region_8.9_spmd, %region_9.10... | conditional | bytes 16777764 | solution.py:470
  159.7 2.9 pack_spare.12
  162.6 1.3 copy-done.10
  163.9 49.8 %exchange_spare.12 = bf16[16,512,256]{2,1,0:T(8,128)(2,1)} custom-call(bf16[16,256,256]{2,1,0:T(8,128)(2,1)} %bitcast.129), custom_call_target="tpu_custom_call" | custom-call | tf_op jit(solution)/shard_map/cond/branch_0_fun/exchange_spare/pallas_call | solution.py:138
  215.7 2.2 copy-done.13
  217.9 23.0 %filter_step.4 = (bf16[64,128,256]{2,1,0:T(8,128)(2,1)S(1)}, bf16[64,128,256]{2,1,0:T(8,128)(2,1)}, f32[256,256]{1,0:T(8,128)S(1)}, f32[8,128]{1,0:T(8,128)S(1)}) custom-call(s32[64]{0:T(128)S(1)} %get-tuple-element.339.source_ref, s32[64]{0:T(128)S(1)} %squeeze.98.send_ref, s32[64]{0:T(128)S(1)} %squeeze.99.spare_ref, bf16[64,128,256]{2,1,0:T(8,128)(2,1)S(1)} %bitcast.132, ...), custom_call_target="tpu_custom_call" | custom-call | flops 3221225472 | bytes 20971520 | tf_op jit(solution)/shard_map/filter_step/pallas_call | solution.py:243
  241.0 2.0 copy-done.16
  243.6 99.9 %exchange_tiles.4 = (bf16[16,512,256]{2,1,0:T(8,128)(2,1)}, bf16[64,128,256]{2,1,0:T(8,128)(2,1)}, bf16[16,16,256]{2,1,0:T(8,128)(2,1)}, f32[16,8,128]{2,1,0:T(8,128)}) custom-call(bf16[16,512,256]{2,1,0:T(8,128)(2,1)} %bitcast.135, bf16[64,128,256]{2,1,0:T(8,128)(2,1)} %get-tuple-element.169.refs_1_, bf16[16,16,256]{2,1,0:T(8,128)(2,1)} %bitcast.160, ...), custom_call_target="tpu_custom_call" | custom-call | tf_op jit(solution)/shard_map/exchange_tiles/pallas_call | solution.py:138
  343.5 67.2 %conditional.4 = (bf16[64,128,256]{2,1,0:T(8,128)(2,1)}) conditional(s32[]{:T(128)} %bitcast.66, (s32[1,16,4]{2,1,0:T(8,128)S(1)}, bf16[64,128,256]{2,1,0:T(8,128)(2,1)}, bf16[64,128,256]{2,1,0:T(8,128)(2,1)}) %tuple.57, (s32[1,16,4]{2,1,0:T(8,128)S(1)}, bf16[64,128,256]{2,1,0:T(8,128)(2,1)}, ...), branch_computations={%region_10.11_spmd, %region_11.12_spmd, %region_12.13_spmd, %regio... | conditional | bytes 16777764 | solution.py:470
  343.8 4.0 pack_spare.17
  347.8 1.6 copy-done.6
  349.4 61.1 %exchange_spare.17 = bf16[16,512,256]{2,1,0:T(8,128)(2,1)} custom-call(bf16[16,384,256]{2,1,0:T(8,128)(2,1)} %bitcast.125), custom_call_target="tpu_custom_call" | custom-call | tf_op jit(solution)/shard_map/cond/branch_1_fun/exchange_spare/pallas_call | solution.py:138
  412.6 2.2 copy-done.14
  414.8 23.0 %filter_step.5 = (bf16[64,128,256]{2,1,0:T(8,128)(2,1)S(1)}, bf16[64,128,256]{2,1,0:T(8,128)(2,1)}, f32[256,256]{1,0:T(8,128)S(1)}, f32[8,128]{1,0:T(8,128)S(1)}) custom-call(s32[64]{0:T(128)S(1)} %get-tuple-element.340.source_ref, s32[64]{0:T(128)S(1)} %squeeze.95.send_ref, s32[64]{0:T(128)S(1)} %squeeze.96.spare_ref, bf16[64,128,256]{2,1,0:T(8,128)(2,1)S(1)} %bitcast.133, ...), custom_call_target="tpu_custom_call" | custom-call | flops 3221225472 | bytes 20971520 | tf_op jit(solution)/shard_map/filter_step/pallas_call | solution.py:243
  437.8 2.0 copy-done.17
  440.5 99.9 %exchange_tiles.5 = (bf16[16,512,256]{2,1,0:T(8,128)(2,1)}, bf16[64,128,256]{2,1,0:T(8,128)(2,1)}, bf16[16,16,256]{2,1,0:T(8,128)(2,1)}, f32[16,8,128]{2,1,0:T(8,128)}) custom-call(bf16[16,512,256]{2,1,0:T(8,128)(2,1)} %bitcast.136, bf16[64,128,256]{2,1,0:T(8,128)(2,1)} %get-tuple-element.175.refs_1_, bf16[16,16,256]{2,1,0:T(8,128)(2,1)} %bitcast.161, ...), custom_call_target="tpu_custom_call" | custom-call | tf_op jit(solution)/shard_map/exchange_tiles/pallas_call | solution.py:138
  540.3 67.0 %conditional.5 = (bf16[64,128,256]{2,1,0:T(8,128)(2,1)}) conditional(s32[]{:T(128)} %bitcast.70, (s32[1,16,4]{2,1,0:T(8,128)S(1)}, bf16[64,128,256]{2,1,0:T(8,128)(2,1)}, bf16[64,128,256]{2,1,0:T(8,128)(2,1)}) %tuple.58, (s32[1,16,4]{2,1,0:T(8,128)S(1)}, bf16[64,128,256]{2,1,0:T(8,128)(2,1)}, ...), branch_computations={%region_14.15_spmd, %region_15.16_spmd, %region_16.17_spmd, %regio... | conditional | bytes 16777764 | solution.py:470
  540.6 4.0 pack_spare.21
  544.6 1.6 copy-done.8
  546.3 61.1 %exchange_spare.21 = bf16[16,512,256]{2,1,0:T(8,128)(2,1)} custom-call(bf16[16,384,256]{2,1,0:T(8,128)(2,1)} %bitcast.127), custom_call_target="tpu_custom_call" | custom-call | tf_op jit(solution)/shard_map/cond/branch_1_fun/exchange_spare/pallas_call | solution.py:138
  607.4 2.2 copy-done.15
  609.5 7.9 %place_tiles.1 = bf16[64,128,256]{2,1,0:T(8,128)(2,1)} custom-call(s32[64]{0:T(128)S(1)} %get-tuple-element.341.source_ref, bf16[64,128,256]{2,1,0:T(8,128)(2,1)S(1)} %bitcast.134, bf16[64,128,256]{2,1,0:T(8,128)(2,1)} %get-tuple-element.353.other_ref), custom_call_target="tpu_custom_call" | custom-call | tf_op jit(solution)/shard_map/place_tiles/pallas_call | solution.py:308
  (121 shorter events, 17.4 us)
Async XLA Ops:
  27.6 2.2 copy-start
  29.8 0.9 copy-start.19
  30.7 0.9 copy-start.21
  31.6 0.7 copy-start.23
  56.1 2.0 copy-start.18
  58.1 0.7 copy-start.27
  159.3 54.5 %copy-start.32 = (f32[16,8,128]{2,1,0:T(8,128)S(1)}, f32[16,8,128]{2,1,0:T(8,128)}, u32[]{:S(2)}) copy-start(f32[16,8,128]{2,1,0:T(8,128)} %get-tuple-element.180) | copy-start | bytes 196612
  159.3 55.7 %copy-start.29 = (bf16[16,16,256]{2,1,0:T(8,128)(2,1)S(1)}, bf16[16,16,256]{2,1,0:T(8,128)(2,1)}, u32[]{:S(2)}) copy-start(bf16[16,16,256]{2,1,0:T(8,128)(2,1)} %get-tuple-element.183) | copy-start | bytes 393220
  159.3 56.4 %copy-start.20 = (bf16[256,256]{1,0:T(8,128)(2,1)S(1)}, bf16[256,256]{1,0:T(8,128)(2,1)}, u32[]{:S(2)}) copy-start(bf16[256,256]{1,0:T(8,128)(2,1)} %refs_2_.5) | copy-start | bytes 393220
  159.3 56.4 %copy-start.22 = (bf16[256,256]{1,0:T(8,128)(2,1)S(1)}, bf16[256,256]{1,0:T(8,128)(2,1)}, u32[]{:S(2)}) copy-start(bf16[256,256]{1,0:T(8,128)(2,1)} %refs_3_.5) | copy-start | bytes 393220
  159.4 56.4 %copy-start.24 = (f32[256]{0:T(256)S(1)}, f32[256]{0:T(256)}, u32[]{:S(2)}) copy-start(f32[256]{0:T(256)} %param.26) | copy-start | bytes 3076
  162.6 1.4 copy-start.10
  215.7 2.2 copy-start.13
  241.0 2.0 copy-start.16
  242.9 0.7 copy-start.25
  343.5 67.2 %copy-start.33 = (f32[16,8,128]{2,1,0:T(8,128)S(1)}, f32[16,8,128]{2,1,0:T(8,128)}, u32[]{:S(2)}) copy-start(f32[16,8,128]{2,1,0:T(8,128)} %get-tuple-element.181) | copy-start | bytes 196612
  343.5 68.4 %copy-start.30 = (bf16[16,16,256]{2,1,0:T(8,128)(2,1)S(1)}, bf16[16,16,256]{2,1,0:T(8,128)(2,1)}, u32[]{:S(2)}) copy-start(bf16[16,16,256]{2,1,0:T(8,128)(2,1)} %get-tuple-element.184) | copy-start | bytes 393220
  347.8 1.6 copy-start.6
  412.6 2.2 copy-start.14
  437.8 2.0 copy-start.17
  439.8 0.7 copy-start.26
  544.6 1.6 copy-start.8
  607.3 2.2 copy-start.15
  609.5 8.0 %copy-start.31 = (f32[16,8,128]{2,1,0:T(8,128)S(1)}, f32[16,8,128]{2,1,0:T(8,128)}, u32[]{:S(2)}) copy-start(f32[16,8,128]{2,1,0:T(8,128)} %get-tuple-element.182) | copy-start | bytes 196612
  609.5 9.8 %copy-start.28 = (bf16[16,16,256]{2,1,0:T(8,128)(2,1)S(1)}, bf16[16,16,256]{2,1,0:T(8,128)(2,1)}, u32[]{:S(2)}) copy-start(bf16[16,16,256]{2,1,0:T(8,128)(2,1)} %get-tuple-element.185) | copy-start | bytes 393220
where the time goes:
time: 628 us; the launch traced here: 621 us
  Pallas kernels  571 us (91%)
  local copies, waits for them, and re-layouts  30.1 us (5%)
  other arithmetic  11.7 us (2%)
  between operations  7.05 us (1%)
    pallas_call x6, Pallas kernels, exchange(): pl.pallas_call(functools.partial(exchange_kernel, islands, kinds), out_sh...  472 us
    pallas_call x3, Pallas kernels, filter_step(): pl.pallas_call(filter_kernel, grid_spec=pltpu.PrefetchScalarGridSpec(num_...  69.9 us
    pallas_call x4, Pallas kernels, place(): pl.pallas_call(place_kernel, grid_spec=pltpu.PrefetchScalarGridSpec(num_s...  18.8 us
    unnamed x48, local copies, waits for them, and re-layouts  17.3 us

commit v1 on v0

--- a/solution.py
+++ b/solution.py
@@ -10,7 +10,7 @@
 TILE = 128
 STEPS = 3
 LANES = 128
-CHUNK = 8
+CHUNK = 16
 MESH = pl.DeviceIdType.MESH
 
 

time: 628 us -> 614 us (0.978); the launches traced: 621 us -> 613 us
  Pallas kernels: 571 us -> 564 us
where the time goes in v1:
time: 614 us; the launch traced here: 613 us
  Pallas kernels  564 us (92%)
  local copies, waits for them, and re-layouts  30.1 us (5%)
  other arithmetic  11.7 us (2%)
  between operations  7.05 us (1%)
    pallas_call x6, Pallas kernels, exchange(): pl.pallas_call(functools.partial(exchange_kernel, islands, kinds), out_sh...  472 us
    pallas_call x3, Pallas kernels, filter_step(): pl.pallas_call(filter_kernel, grid_spec=pltpu.PrefetchScalarGridSpec(num_...  64.9 us
    unnamed x48, local copies, waits for them, and re-layouts  17.3 us
    pallas_call x4, Pallas kernels, place(): pl.pallas_call(place_kernel, grid_spec=pltpu.PrefetchScalarGridSpec(num_s...  16.5 us

profile of v1, /device:TPU:13, one launch (start us, length us, event | category | flops | bytes accessed | tf_op | source)
XLA Modules:
  0.0 613.2 jit_solution(692860837090785983)
XLA Ops:
  3.7 10.3 %share_tables.1 = s32[32,8,128]{2,1,0:T(8,128)} custom-call(s32[8,128]{1,0:T(8,128)} %pad.8.table_ref), custom_call_target="tpu_custom_call" | custom-call | tf_op jit(solution)/shard_map/share_tables/pallas_call | solution.py:65
  14.8 0.9 slice.166
  16.7 1.7 convert_reduce_fusion
  26.1 0.9 select_reduce_fusion
  27.6 2.2 copy-done
  29.8 0.9 copy-done.19
  30.7 0.9 copy-done.21
  32.3 22.1 %filter_step.3 = (bf16[64,128,256]{2,1,0:T(8,128)(2,1)S(1)}, bf16[64,128,256]{2,1,0:T(8,128)(2,1)}, f32[256,256]{1,0:T(8,128)S(1)}, f32[8,128]{1,0:T(8,128)S(1)}) custom-call(s32[64]{0:T(128)S(1)} %iota.50.source_ref, s32[64]{0:T(128)S(1)} %squeeze.100.send_ref, s32[64]{0:T(128)S(1)} %squeeze.101.spare_ref, bf16[64,128,256]{2,1,0:T(8,128)(2,1)S(1)} %bitcast.118, ...), custom_call_target="tpu_custom_call" | custom-call | flops 3221225472 | bytes 20971520 | tf_op jit(solution)/shard_map/filter_step/pallas_call | solution.py:243
  54.4 2.0 copy-done.18
  57.1 100.6 %exchange_tiles.3 = (bf16[16,512,256]{2,1,0:T(8,128)(2,1)}, bf16[64,128,256]{2,1,0:T(8,128)(2,1)}, bf16[16,16,256]{2,1,0:T(8,128)(2,1)}, f32[16,8,128]{2,1,0:T(8,128)}) custom-call(bf16[16,512,256]{2,1,0:T(8,128)(2,1)} %bitcast.137, bf16[64,128,256]{2,1,0:T(8,128)(2,1)} %get-tuple-element.163.refs_1_, bf16[16,16,256]{2,1,0:T(8,128)(2,1)} %bitcast.159, ...), custom_call_target="tpu_custom_call" | custom-call | tf_op jit(solution)/shard_map/exchange_tiles/pallas_call | solution.py:138
  157.7 53.7 %conditional.3 = (bf16[64,128,256]{2,1,0:T(8,128)(2,1)}) conditional(s32[]{:T(128)} %bitcast.62, (s32[1,16,4]{2,1,0:T(8,128)S(1)}, bf16[64,128,256]{2,1,0:T(8,128)(2,1)}, bf16[64,128,256]{2,1,0:T(8,128)(2,1)}) %tuple.56, (s32[1,16,4]{2,1,0:T(8,128)S(1)}, bf16[64,128,256]{2,1,0:T(8,128)(2,1)}, ...), branch_computations={%region_6.7_spmd, %region_7.8_spmd, %region_8.9_spmd, %region_9.10... | conditional | bytes 16777764 | solution.py:470
  158.0 2.2 pack_spare.12
  160.2 1.3 copy-done.10
  161.6 49.8 %exchange_spare.12 = bf16[16,512,256]{2,1,0:T(8,128)(2,1)} custom-call(bf16[16,256,256]{2,1,0:T(8,128)(2,1)} %bitcast.129), custom_call_target="tpu_custom_call" | custom-call | tf_op jit(solution)/shard_map/cond/branch_0_fun/exchange_spare/pallas_call | solution.py:138
  213.4 2.2 copy-done.13
  215.5 21.3 %filter_step.4 = (bf16[64,128,256]{2,1,0:T(8,128)(2,1)S(1)}, bf16[64,128,256]{2,1,0:T(8,128)(2,1)}, f32[256,256]{1,0:T(8,128)S(1)}, f32[8,128]{1,0:T(8,128)S(1)}) custom-call(s32[64]{0:T(128)S(1)} %get-tuple-element.339.source_ref, s32[64]{0:T(128)S(1)} %squeeze.98.send_ref, s32[64]{0:T(128)S(1)} %squeeze.99.spare_ref, bf16[64,128,256]{2,1,0:T(8,128)(2,1)S(1)} %bitcast.132, ...), custom_call_target="tpu_custom_call" | custom-call | flops 3221225472 | bytes 20971520 | tf_op jit(solution)/shard_map/filter_step/pallas_call | solution.py:243
  236.9 2.0 copy-done.16
  239.5 99.9 %exchange_tiles.4 = (bf16[16,512,256]{2,1,0:T(8,128)(2,1)}, bf16[64,128,256]{2,1,0:T(8,128)(2,1)}, bf16[16,16,256]{2,1,0:T(8,128)(2,1)}, f32[16,8,128]{2,1,0:T(8,128)}) custom-call(bf16[16,512,256]{2,1,0:T(8,128)(2,1)} %bitcast.135, bf16[64,128,256]{2,1,0:T(8,128)(2,1)} %get-tuple-element.169.refs_1_, bf16[16,16,256]{2,1,0:T(8,128)(2,1)} %bitcast.160, ...), custom_call_target="tpu_custom_call" | custom-call | tf_op jit(solution)/shard_map/exchange_tiles/pallas_call | solution.py:138
  339.4 66.3 %conditional.4 = (bf16[64,128,256]{2,1,0:T(8,128)(2,1)}) conditional(s32[]{:T(128)} %bitcast.66, (s32[1,16,4]{2,1,0:T(8,128)S(1)}, bf16[64,128,256]{2,1,0:T(8,128)(2,1)}, bf16[64,128,256]{2,1,0:T(8,128)(2,1)}) %tuple.57, (s32[1,16,4]{2,1,0:T(8,128)S(1)}, bf16[64,128,256]{2,1,0:T(8,128)(2,1)}, ...), branch_computations={%region_10.11_spmd, %region_11.12_spmd, %region_12.13_spmd, %regio... | conditional | bytes 16777764 | solution.py:470
  339.7 3.1 pack_spare.17
  342.9 1.6 copy-done.6
  344.5 61.1 %exchange_spare.17 = bf16[16,512,256]{2,1,0:T(8,128)(2,1)} custom-call(bf16[16,384,256]{2,1,0:T(8,128)(2,1)} %bitcast.125), custom_call_target="tpu_custom_call" | custom-call | tf_op jit(solution)/shard_map/cond/branch_1_fun/exchange_spare/pallas_call | solution.py:138
  407.7 2.2 copy-done.14
  409.9 21.4 %filter_step.5 = (bf16[64,128,256]{2,1,0:T(8,128)(2,1)S(1)}, bf16[64,128,256]{2,1,0:T(8,128)(2,1)}, f32[256,256]{1,0:T(8,128)S(1)}, f32[8,128]{1,0:T(8,128)S(1)}) custom-call(s32[64]{0:T(128)S(1)} %get-tuple-element.340.source_ref, s32[64]{0:T(128)S(1)} %squeeze.95.send_ref, s32[64]{0:T(128)S(1)} %squeeze.96.spare_ref, bf16[64,128,256]{2,1,0:T(8,128)(2,1)S(1)} %bitcast.133, ...), custom_call_target="tpu_custom_call" | custom-call | flops 3221225472 | bytes 20971520 | tf_op jit(solution)/shard_map/filter_step/pallas_call | solution.py:243
  431.3 2.0 copy-done.17
  433.9 99.8 %exchange_tiles.5 = (bf16[16,512,256]{2,1,0:T(8,128)(2,1)}, bf16[64,128,256]{2,1,0:T(8,128)(2,1)}, bf16[16,16,256]{2,1,0:T(8,128)(2,1)}, f32[16,8,128]{2,1,0:T(8,128)}) custom-call(bf16[16,512,256]{2,1,0:T(8,128)(2,1)} %bitcast.136, bf16[64,128,256]{2,1,0:T(8,128)(2,1)} %get-tuple-element.175.refs_1_, bf16[16,16,256]{2,1,0:T(8,128)(2,1)} %bitcast.161, ...), custom_call_target="tpu_custom_call" | custom-call | tf_op jit(solution)/shard_map/exchange_tiles/pallas_call | solution.py:138
  533.7 66.2 %conditional.5 = (bf16[64,128,256]{2,1,0:T(8,128)(2,1)}) conditional(s32[]{:T(128)} %bitcast.70, (s32[1,16,4]{2,1,0:T(8,128)S(1)}, bf16[64,128,256]{2,1,0:T(8,128)(2,1)}, bf16[64,128,256]{2,1,0:T(8,128)(2,1)}) %tuple.58, (s32[1,16,4]{2,1,0:T(8,128)S(1)}, bf16[64,128,256]{2,1,0:T(8,128)(2,1)}, ...), branch_computations={%region_14.15_spmd, %region_15.16_spmd, %region_16.17_spmd, %regio... | conditional | bytes 16777764 | solution.py:470
  534.0 3.1 pack_spare.21
  537.2 1.6 copy-done.8
  538.8 61.1 %exchange_spare.21 = bf16[16,512,256]{2,1,0:T(8,128)(2,1)} custom-call(bf16[16,384,256]{2,1,0:T(8,128)(2,1)} %bitcast.127), custom_call_target="tpu_custom_call" | custom-call | tf_op jit(solution)/shard_map/cond/branch_1_fun/exchange_spare/pallas_call | solution.py:138
  599.9 2.2 copy-done.15
  602.1 8.0 %place_tiles.1 = bf16[64,128,256]{2,1,0:T(8,128)(2,1)} custom-call(s32[64]{0:T(128)S(1)} %get-tuple-element.341.source_ref, bf16[64,128,256]{2,1,0:T(8,128)(2,1)S(1)} %bitcast.134, bf16[64,128,256]{2,1,0:T(8,128)(2,1)} %get-tuple-element.353.other_ref), custom_call_target="tpu_custom_call" | custom-call | tf_op jit(solution)/shard_map/place_tiles/pallas_call | solution.py:308
  (121 shorter events, 17.4 us)
Async XLA Ops:
  27.6 2.2 copy-start
  29.8 0.9 copy-start.19
  30.7 0.9 copy-start.21
  31.6 0.7 copy-start.23
  54.4 2.0 copy-start.18
  56.4 0.7 copy-start.27
  157.7 53.8 %copy-start.32 = (f32[16,8,128]{2,1,0:T(8,128)S(1)}, f32[16,8,128]{2,1,0:T(8,128)}, u32[]{:S(2)}) copy-start(f32[16,8,128]{2,1,0:T(8,128)} %get-tuple-element.180) | copy-start | bytes 196612
  157.7 55.0 %copy-start.29 = (bf16[16,16,256]{2,1,0:T(8,128)(2,1)S(1)}, bf16[16,16,256]{2,1,0:T(8,128)(2,1)}, u32[]{:S(2)}) copy-start(bf16[16,16,256]{2,1,0:T(8,128)(2,1)} %get-tuple-element.183) | copy-start | bytes 393220
  157.7 55.6 %copy-start.20 = (bf16[256,256]{1,0:T(8,128)(2,1)S(1)}, bf16[256,256]{1,0:T(8,128)(2,1)}, u32[]{:S(2)}) copy-start(bf16[256,256]{1,0:T(8,128)(2,1)} %refs_2_.5) | copy-start | bytes 393220
  157.7 55.6 %copy-start.22 = (bf16[256,256]{1,0:T(8,128)(2,1)S(1)}, bf16[256,256]{1,0:T(8,128)(2,1)}, u32[]{:S(2)}) copy-start(bf16[256,256]{1,0:T(8,128)(2,1)} %refs_3_.5) | copy-start | bytes 393220
  157.7 55.6 %copy-start.24 = (f32[256]{0:T(256)S(1)}, f32[256]{0:T(256)}, u32[]{:S(2)}) copy-start(f32[256]{0:T(256)} %param.26) | copy-start | bytes 3076
  160.2 1.4 copy-start.10
  213.3 2.2 copy-start.13
  236.9 2.0 copy-start.16
  238.9 0.7 copy-start.25
  339.4 66.4 %copy-start.33 = (f32[16,8,128]{2,1,0:T(8,128)S(1)}, f32[16,8,128]{2,1,0:T(8,128)}, u32[]{:S(2)}) copy-start(f32[16,8,128]{2,1,0:T(8,128)} %get-tuple-element.181) | copy-start | bytes 196612
  339.4 67.6 %copy-start.30 = (bf16[16,16,256]{2,1,0:T(8,128)(2,1)S(1)}, bf16[16,16,256]{2,1,0:T(8,128)(2,1)}, u32[]{:S(2)}) copy-start(bf16[16,16,256]{2,1,0:T(8,128)(2,1)} %get-tuple-element.184) | copy-start | bytes 393220
  342.9 1.6 copy-start.6
  407.7 2.2 copy-start.14
  431.3 2.0 copy-start.17
  433.3 0.7 copy-start.26
  537.2 1.6 copy-start.8
  599.9 2.2 copy-start.15
  602.1 8.0 %copy-start.31 = (f32[16,8,128]{2,1,0:T(8,128)S(1)}, f32[16,8,128]{2,1,0:T(8,128)}, u32[]{:S(2)}) copy-start(f32[16,8,128]{2,1,0:T(8,128)} %get-tuple-element.182) | copy-start | bytes 196612
  602.1 9.8 %copy-start.28 = (bf16[16,16,256]{2,1,0:T(8,128)(2,1)S(1)}, bf16[16,16,256]{2,1,0:T(8,128)(2,1)}, u32[]{:S(2)}) copy-start(bf16[16,16,256]{2,1,0:T(8,128)(2,1)} %get-tuple-element.185) | copy-start | bytes 393220
